TPU v7x, 32 devices: a whole 2x2x4 slice. The times are simulated.
32 devices in a mesh: grp: 2 (over x), row: 8 (over z, y), col: 2 (over core).
Axes of the slice: x: 2, y: 2, z: 4, core: 2. Of those that a mesh axis runs over, the one named last changes fastest.
Arguments:
- pair: bfloat16 [128, 64, 128], P(('grp', 'row'), 'col'), parts along dimension 0, may hold values from -6 to 6
- token_mask: int32 [128], P('grp'), parts along dimension 0, may hold values 0 or 1
- chain_ids: int32 [128], P('grp'), parts along dimension 0, may hold values from 0 to 5, as said below
- chain_bias: float32 [128], replicated, may hold values from -4 to 4
- in_gain: float32 [2, 128], replicated, may hold values from 0.5 to 2
- proj_weight: bfloat16 [2, 128, 640], replicated, may hold values from -0.5 to 0.5
- out_gain: float32 [2, 128], replicated, may hold values from 0.5 to 2
- out_weight: bfloat16 [2, 128, 128], replicated, may hold values from -0.5 to 0.5
Outputs:
- updated: bfloat16 [128, 64, 128], P(('grp', 'row'), 'col'), parts along dimension 0
There are 2 independent parts, one for each index of `grp`. A program takes and returns all parts, laid end to end along the dimension named above; an argument that names none is the same for every part. Nothing has to cross between parts.
Inputs may be any that keep to these rules, and one draw needn't show every extreme that they name: `chain_ids`: chain ids never fall along the tokens; there are exactly six chains, each of at least one token.
All inputs are finite; a program needn't handle non-finite values.
Results may differ from a plain program's by a relative error of at most 0.012.
Values may be sent and summed in bfloat16 or wider, within the bound.
A program may use at most 64 MiB of HBM per device.

v0:
```python
import jax
import jax.numpy as jnp
from jax import lax
from jax.sharding import PartitionSpec as P


def broadcast(shard, axis, root):
    mine = lax.axis_index(axis) == root
    return lax.psum(jnp.where(mine, shard, jnp.zeros_like(shard)), axis)


def layer_norm(values, gain):
    mean = jnp.mean(values, axis=-1, keepdims=True)
    centred = values - mean
    variance = jnp.mean(centred * centred, axis=-1, keepdims=True)
    return centred * lax.rsqrt(variance + 1e-05) * gain


def project(state, pmask, gain_in, weight_in, hidden):
    rows, cols, width = state.shape
    normed = layer_norm(state, gain_in).astype(jnp.bfloat16)
    proj = jnp.dot(
        normed.reshape(-1, width), weight_in, preferred_element_type=jnp.float32
    ).reshape(rows, cols, -1)
    a_side = (
        pmask[:, :, None] * jax.nn.sigmoid(proj[:, :, hidden : 2 * hidden]) * proj[:, :, :hidden]
    ).astype(jnp.bfloat16)
    b_side = (
        pmask[:, :, None]
        * jax.nn.sigmoid(proj[:, :, 3 * hidden : 4 * hidden])
        * proj[:, :, 2 * hidden : 3 * hidden]
    ).astype(jnp.bfloat16)
    gate = jax.nn.sigmoid(proj[:, :, 4 * hidden :])
    return (a_side, b_side, gate)


def finish(state, mixed, gate, gain_out, weight_out):
    rows, cols, width = state.shape
    hidden = weight_out.shape[0]
    mnorm = layer_norm(mixed, gain_out).astype(jnp.bfloat16)
    change = jnp.dot(
        mnorm.reshape(-1, hidden), weight_out, preferred_element_type=jnp.float32
    ).reshape(rows, cols, width)
    return (state + gate * change).astype(jnp.bfloat16)


def shards(pair, token_mask, chain_ids, chain_bias, in_gain, proj_weight, out_gain, out_weight):
    rows, cols, width = pair.shape
    hidden = out_weight.shape[1]
    row_start = lax.axis_index("row") * rows
    col_start = lax.axis_index("col") * cols
    mask_rows = lax.dynamic_slice_in_dim(token_mask, row_start, rows).astype(jnp.float32)
    mask_cols = lax.dynamic_slice_in_dim(token_mask, col_start, cols).astype(jnp.float32)
    chain_rows = lax.dynamic_slice_in_dim(chain_ids, row_start, rows)
    chain_cols = lax.dynamic_slice_in_dim(chain_ids, col_start, cols)
    pmask = mask_rows[:, None] * mask_cols[None, :]
    same = (chain_rows[:, None] == chain_cols[None, :]).astype(jnp.float32)
    start = pair.astype(jnp.float32) + same[:, :, None] * chain_bias
    a_out, b_out, gate_out = project(start, pmask, in_gain[0], proj_weight[0], hidden)
    partial_sums = jnp.einsum(
        "ikh,jkh->ijh",
        a_out,
        lax.all_gather(b_out, "row", axis=0, tiled=True),
        preferred_element_type=jnp.float32,
    )
    mixed_out = lax.psum_scatter(partial_sums, "col", scatter_dimension=1, tiled=True)
    first = finish(start, mixed_out, gate_out, out_gain[0], out_weight[0])
    state = first.astype(jnp.float32)
    a_in, b_in, gate_in = project(state, pmask, in_gain[1], proj_weight[1], hidden)
    column_block = lax.all_gather(a_in, "row", axis=0, tiled=True)
    owner = row_start // cols
    offset = jnp.clip(row_start - col_start, 0, cols - rows)
    picked = lax.dynamic_slice_in_dim(column_block, offset, rows, 1)
    panel = broadcast(picked, "col", owner)
    mixed_in = jnp.einsum(
        "kih,kjh->ijh",
        panel,
        lax.all_gather(b_in, "row", axis=0, tiled=True),
        preferred_element_type=jnp.float32,
    )
    return finish(state, mixed_in, gate_in, out_gain[1], out_weight[1])


def solution(mesh):
    in_specs = (P(("grp", "row"), "col", None), P("grp"), P("grp"), P(), P(), P(), P(), P())
    out_specs = P(("grp", "row"), "col", None)
    return jax.shard_map(shards, mesh=mesh, in_specs=in_specs, out_specs=out_specs, check_vma=False)
```

profile of v0, /device:TPU:0, one launch (start us, length us, event | category | flops | bytes accessed | tf_op | source)
XLA Modules:
  0.0 143.1 jit_solution(3583891203361170622)
XLA Ops:
  6.5 0.0 reduce-scatter.2.cloned.1.call-start
  6.5 0.7 dynamic-slice_convert_fusion
  7.3 0.7 dynamic_slice.16
  8.0 0.7 dynamic-slice_convert_fusion.1
  8.7 0.7 dynamic_slice.15
  9.5 0.8 slice_bitcast_fusion.1
  10.2 0.1 compare_convert_fusion
  10.3 1.0 fusion.39
  11.3 1.1 multiply_reduce_fusion.3
  12.4 0.1 broadcast_multiply_fusion
  12.5 1.3 fusion.8
  13.8 0.1 fusion.25
  13.9 0.2 copy.38
  14.1 33.0 %all_gather.9 = bf16[64,32,128]{2,1,0:T(8,128)(2,1)S(1)} all-gather(bf16[8,32,128]{2,1,0:T(8,128)(2,1)S(1)} %get-tuple-element.8), channel_id=1, replica_groups=mesh['grp'=2,'row'=8,'col'=2] {'row'}, dimensions={0}, use_global_device_ids=true | all-gather | bytes 589824 | tf_op jit(solution)/shard_map/all_gather | solution.py:63
  47.1 3.0 %copy.37 = bf16[64,32,128]{1,0,2:T(8,128)(2,1)S(1)} copy(bf16[64,32,128]{2,1,0:T(8,128)(2,1)S(1)} %all_gather.9) | data formatting | bytes 1048576 | tf_op jit(solution)/shard_map/all_gather | solution.py:63
  50.0 0.0 copy-start.1
  50.1 1.2 convolution_bitcast_fusion.1
  51.2 0.0 copy-start
  51.2 0.9 copy.39
  52.2 0.0 reduce-scatter.2.cloned.1.call-update
  52.2 0.0 all-reduce.2.cloned.1.call-start
  52.3 0.8 slice_bitcast_fusion
  53.0 8.1 %reduce-scatter.2.cloned.1.call-done = f32[8,32,128]{2,0,1:T(8,128)} async-done(((f32[8,64,128]{2,0,1:T(8,128)}), f32[8,32,128]{2,0,1:T(8,128)}) %reduce-scatter.2.cloned.1.call-update) | async-done | bytes 131088 | tf_op jit(solution)/shard_map/reduce_scatter | solution.py:66
  61.1 1.0 reduce_sum.74
  62.1 0.1 copy.40
  62.2 0.1 copy.41
  62.3 1.1 multiply_reduce_fusion.2
  63.4 0.1 copy.42
  63.4 0.1 copy.43
  63.5 1.0 multiply_convert_fusion.2
  64.6 0.0 copy-done.1
  64.6 1.1 fusion.53
  65.7 0.2 multiply_reduce_fusion.1
  65.9 0.0 copy-done
  65.9 0.3 fusion.6
  66.2 0.1 fusion.12
  66.3 31.8 %all_gather.11 = bf16[64,32,128]{2,1,0:T(8,128)(2,1)S(1)} all-gather(bf16[8,32,128]{2,1,0:T(8,128)(2,1)S(1)} %get-tuple-element.5), channel_id=1, replica_groups=mesh['grp'=2,'row'=8,'col'=2] {'row'}, dimensions={0}, use_global_device_ids=true | all-gather | bytes 589824 | tf_op jit(solution)/shard_map/all_gather | solution.py:70
  98.1 0.1 constant_dynamic-slice_fusion
  98.2 0.2 copy.48
  98.4 0.7 broadcast_select_fusion
  99.1 0.0 all-reduce.2.cloned.1.call-update
  99.2 31.2 %all_gather.10 = bf16[64,32,128]{2,1,0:T(8,128)(2,1)S(1)} all-gather(bf16[8,32,128]{2,1,0:T(8,128)(2,1)S(1)} %get-tuple-element.6), channel_id=1, replica_groups=mesh['grp'=2,'row'=8,'col'=2] {'row'}, dimensions={0}, use_global_device_ids=true | all-gather | bytes 589824 | tf_op jit(solution)/shard_map/all_gather | solution.py:78
  130.3 3.0 %copy.46 = bf16[64,32,128]{1,0,2:T(8,128)(2,1)S(1)} copy(bf16[64,32,128]{2,1,0:T(8,128)(2,1)S(1)} %all_gather.10) | data formatting | bytes 1048576 | tf_op jit(solution)/shard_map/all_gather | solution.py:78
  133.3 0.0 copy-start.2
  133.3 0.0 all-reduce.2.cloned.1.call-done
  133.4 1.6 %fusion.54 = (f32[8,32]{1,0:T(8,128)S(1)}, f32[8,32,128]{1,0,2:T(8,128)S(1)}) fusion(bf16[64,32,128]{1,0,2:T(8,128)(2,1)S(1)} %copy.46, bf16[64,8,128]{0,1,2:T(8,128)(2,1)} %all-reduce.2.cloned.1.call-done), kind=kOutput, calls=%fused_computation.95 | convolution fusion | flops 4226816 | bytes 787456 | tf_op jit(solution)/shard_map/kih,kjh->ijh/dot_general | solution.py:75
  135.0 0.1 multiply_reduce_fusion
  135.1 0.2 multiply_convert_fusion
  135.3 0.0 copy-done.2
  135.4 0.9 fusion.3
  (8 shorter events, 0.0 us)
Async XLA Ops:
  6.5 54.6 %reduce-scatter.2.cloned.1.call-start = ((), (), s32[]{:S(2)}) async-start(), calls=%async_computation.1 | async-start | bytes 393216 | tf_op jit(solution)/shard_map/reduce_scatter | solution.py:66
  50.0 14.5 %copy-start.1 = (f32[128]{0:T(128)S(1)}, f32[128]{0:T(128)}, u32[]{:S(2)}) copy-start(f32[128]{0:T(128)} %param.11) | copy-start | bytes 1540
  51.2 14.7 %copy-start = (bf16[2,128,640]{2,1,0:T(8,128)(2,1)S(1)}, bf16[2,128,640]{2,1,0:T(8,128)(2,1)}, u32[]{:S(2)}) copy-start(bf16[2,128,640]{2,1,0:T(8,128)(2,1)} %param.13) | copy-start | bytes 983044
  52.2 81.2 %all-reduce.2.cloned.1.call-start = ((), (), s32[]{:S(2)}) async-start(), calls=%async_computation.2 | async-start | bytes 524288 | tf_op jit(solution)/shard_map/psum | solution.py:9
  133.3 2.0 %copy-start.2 = (bf16[2,128,128]{2,1,0:T(8,128)(2,1)S(1)}, bf16[2,128,128]{2,1,0:T(8,128)(2,1)}, u32[]{:S(2)}) copy-start(bf16[2,128,128]{2,1,0:T(8,128)(2,1)} %param.15) | copy-start | bytes 196612
Sparse Core Ops, SparseCore 0:
  52.3 8.7 reduce-scatter.1
  99.3 19.0 all-reduce.1
where the time goes:
time: 143 us
  blocking collectives  96 us (67%)
  between operations  13.6 us (10%)
  local copies, waits for them, and re-layouts  10.6 us (7%)
  other arithmetic  8.32 us (6%)
  waiting for transfers between devices  8.15 us (6%)
  matrix products  6.33 us (4%)
    all_gather x1, blocking collectives, shards(): lax.all_gather(b_out, 'row', axis=0, tiled=True)  33 us
    all_gather x1, blocking collectives, shards(): column_block = lax.all_gather(a_in, 'row', axis=0, tiled=True)  31.8 us
    all_gather x1, blocking collectives, shards(): lax.all_gather(b_in, 'row', axis=0, tiled=True)  31.2 us
    reduce_scatter x1, waiting for transfers between devices, shards(): lax.psum_scatter(partial_sums, 'col', scatter_dimension=1, tiled=True)  8.09 us
    all_gather x1, local copies, waits for them, and re-layouts, shards(): lax.all_gather(b_out, 'row', axis=0, tiled=True)  2.97 us
    all_gather x1, local copies, waits for them, and re-layouts, shards(): lax.all_gather(b_in, 'row', axis=0, tiled=True)  2.97 us
  transfers between devices with their start and end apart: 2, of which 1 were waited for; matrix products, arithmetic and copies ran while one was open for 3% of the time, Pallas kernels for 0%

commit v1 on v0

v1 whole, which is shorter than its diff:
```python
import functools
import jax
import jax.numpy as jnp
from jax import lax
from jax.experimental import pallas as pl
from jax.experimental.pallas import tpu as pltpu
from jax.sharding import PartitionSpec as P

F32 = jnp.float32
BF16 = jnp.bfloat16
MESH = pl.DeviceIdType.MESH


def sigmoid(x):
    return 0.5 * jnp.tanh(0.5 * x) + 0.5


def layer_norm(values, gain):
    mean = jnp.mean(values, axis=-1, keepdims=True)
    centred = values - mean
    variance = jnp.mean(centred * centred, axis=-1, keepdims=True)
    return centred * lax.rsqrt(variance + 1e-05) * gain


def kernel(
    nrow,
    pair_ref, mask_ref, chain_ref, bias_ref, gin_ref, wp_ref, gout_ref, wo_ref,
    out_ref,
    state, pm, gate, mixed, own_b, own_a, a1, a1f, b1, part, a2s, a2, b2,
    s_b1, s_f1, r_b1, s_a1, r_a1, s_a2, s_fa2, r_a2, s_b2, s_f2, r_b2,
):
    rows, cols, width = pair_ref.shape
    hidden = wo_ref.shape[1]
    nz = nrow // 2
    half = nrow // 2
    grp = lax.axis_index("grp")
    r = lax.axis_index("row")
    c = lax.axis_index("col")
    z, y = r // 2, r % 2
    rn = z * 2 + (1 - y)
    tokens = rows * cols
    d = r // half
    q_me = r % half

    def send(src, dst, ss, rs, row, col):
        return pltpu.make_async_remote_copy(
            src_ref=src, dst_ref=dst, send_sem=ss, recv_sem=rs,
            device_id=(grp, row, col), device_id_type=MESH,
        )

    barrier = pltpu.get_barrier_semaphore()
    for k in range(1, 2 * nrow):
        t = lax.rem(r * 2 + c + k, 2 * nrow)
        pl.semaphore_signal(barrier, inc=1, device_id=(grp, t // 2, t % 2), device_id_type=MESH)

    lane_rows = lax.broadcasted_iota(jnp.int32, (8, width), 0)
    for jb in range(cols // 8):
        mcol = jnp.zeros((8, width), jnp.int32)
        ccol = jnp.zeros((8, width), jnp.int32)
        for s in range(8):
            at = c * cols + jb * 8 + s
            mcol = jnp.where(lane_rows == s, mask_ref[at], mcol)
            ccol = jnp.where(lane_rows == s, chain_ref[at], ccol)
        mcol = mcol.astype(F32)
        js = slice(jb * 8, jb * 8 + 8)
        for i in range(rows):
            mi = mask_ref[r * rows + i].astype(F32)
            pm[i, js] = mcol * mi
            same = (ccol == chain_ref[r * rows + i]).astype(F32)
            state[i, js] = pair_ref[i, js].astype(F32) + same * bias_ref[...]

    def normed_of(l):
        zs = state[...].reshape(tokens, width)
        return layer_norm(zs, gin_ref[l : l + 1, :]).astype(BF16)

    def side(normed, l, at):
        pr = jnp.dot(normed, wp_ref[l, :, at : at + 2 * hidden], preferred_element_type=F32)
        return pm[...].reshape(tokens, width) * sigmoid(pr[:, hidden:]) * pr[:, :hidden]

    def gate_of(normed, l):
        pr = jnp.dot(normed, wp_ref[l, :, 4 * hidden :], preferred_element_type=F32)
        gate[...] = sigmoid(pr)

    def finish(l):
        mn = layer_norm(mixed[...].reshape(tokens, hidden), gout_ref[l : l + 1, :]).astype(BF16)
        change = jnp.dot(mn, wo_ref[l], preferred_element_type=F32)
        res = state[...].reshape(tokens, width) + gate[...] * change
        return res.astype(BF16)

    normed = normed_of(0)
    own_b[...] = side(normed, 0, 2 * hidden).astype(BF16).reshape(rows, cols, hidden)
    pl.semaphore_wait(barrier, 2 * nrow - 1)

    b_sends = []
    for dz in range(1, nz):
        tz = lax.rem(z + dz, nz)
        cp = send(own_b, b1.at[q_me, c], s_b1.at[dz], r_b1.at[q_me, c], tz * 2 + y, d)
        cp.start()
        b_sends.append(cp)
    sib_b = send(own_b, b1.at[q_me, c], s_b1.at[0], r_b1.at[q_me, c], r, 1 - c)

    @pl.when(d != c)
    def _():
        sib_b.start()

    @pl.when(d == c)
    def _():
        b1[q_me, c] = own_b[...]

    a1[c] = side(normed, 0, 0).astype(BF16).reshape(rows, cols, hidden)
    a_send = send(a1.at[c], a1.at[c], s_a1, r_a1, r, 1 - c)
    a_send.start()
    gate_of(normed, 0)

    f_sends = []
    for t in range(nz // 2):
        q = t * 2 + y
        mine = (c * (nz // 2) + t) == z
        for cc in range(2):
            @pl.when(jnp.logical_not(jnp.logical_and(mine, c == cc)))
            def _():
                send(b1.at[q, cc], b1.at[q, cc], s_b1.at[0], r_b1.at[q, cc], rn, c).wait_recv()
            cp = send(b1.at[q, cc], b1.at[q, cc], s_f1.at[t, cc], r_b1.at[q, cc], rn, c)
            cp.start()
            f_sends.append(cp)
        if t == 0:
            send(a1.at[1 - c], a1.at[1 - c], s_a1, r_a1, r, 1 - c).wait_recv()
            for cc in range(2):
                a1f[:, cc * cols : (cc + 1) * cols, :] = a1[cc].astype(F32)

    kb_n = 2 * cols // 8

    def outgoing(q):
        def body(j, carry):
            b0 = b1[q, 0, j].astype(F32)
            bb1 = b1[q, 1, j].astype(F32)
            bs = [b0[kb * 8 : kb * 8 + 8] for kb in range(kb_n // 2)]
            bs += [bb1[kb * 8 : kb * 8 + 8] for kb in range(kb_n // 2)]
            base = pl.multiple_of((q * rows + j) * (rows * 8), rows * 8)
            for i in range(rows):
                acc = a1f[i, 0:8] * bs[0]
                for kb in range(1, kb_n):
                    acc = acc + a1f[i, kb * 8 : kb * 8 + 8] * bs[kb]
                part[pl.ds(base + i * 8, 8), :] = acc
            return carry
        lax.fori_loop(0, rows, body, 0)

    for t in range(nz // 2):
        outgoing(t * 2 + y)
    for t in range(nz // 2):
        q = t * 2 + (1 - y)
        for cc in range(2):
            send(b1.at[q, cc], b1.at[q, cc], s_f1.at[t, cc], r_b1.at[q, cc], rn, c).wait_recv()
        outgoing(q)
    for i in range(rows):
        tot = part[pl.ds(i * 8, cols, stride=rows * 8), :]
        for s in range(1, 8):
            tot = tot + part[pl.ds(i * 8 + s, cols, stride=rows * 8), :]
        mixed[i] = tot
    state[...] = finish(0).astype(F32).reshape(rows, cols, width)

    normed = normed_of(1)
    a_side = side(normed, 1, 0).reshape(rows, cols, hidden)
    for q in range(half):
        a2s[q] = a_side[:, q * rows : (q + 1) * rows, :].reshape(rows * rows, hidden).astype(BF16)
    a_sends = []
    for k in range(half):
        q = lax.rem(q_me + k, half)
        tr = c * half + q
        cp = send(a2s.at[q], a2.at[r], s_a2.at[k], r_a2.at[r], tr, y)
        local = jnp.logical_and(tr == r, y == c)

        @pl.when(jnp.logical_not(local))
        def _():
            cp.start()

        @pl.when(local)
        def _():
            a2[r] = a2s[q]
        a_sends.append((cp, local))
    b2[r] = side(normed, 1, 2 * hidden).astype(BF16).reshape(rows, cols, hidden)
    b2_sends = []
    for dz in range(1, nz):
        tz = lax.rem(z + dz, nz)
        cp = send(b2.at[r], b2.at[r], s_b2.at[dz], r_b2.at[r], tz * 2 + y, c)
        cp.start()
        b2_sends.append(cp)
    cp = send(b2.at[r], b2.at[r], s_f2.at[0], r_b2.at[r], rn, c)
    cp.start()
    b2_sends.append(cp)
    gate_of(normed, 1)

    for t in range(nz):
        zz = lax.rem(z + t, nz)
        rr = zz * 2 + c
        @pl.when(jnp.logical_not(jnp.logical_and(rr == r, d == c)))
        def _():
            send(a2.at[rr], a2.at[rr], s_a2.at[0], r_a2.at[rr], r, 1 - c).wait_recv()
        cp = send(a2.at[rr], a2.at[rr], s_fa2.at[t], r_a2.at[rr], r, 1 - c)
        cp.start()
        b2_sends.append(cp)
    for t in range(nz):
        rr = lax.rem(z + t, nz) * 2 + (1 - c)
        send(a2.at[rr], a2.at[rr], s_fa2.at[t], r_a2.at[rr], r, 1 - c).wait_recv()

    jw = min(cols, 32)

    def incoming(rr, first):
        af = a2[rr].astype(F32)
        for jb in range(cols // jw):
            js = slice(jb * jw, (jb + 1) * jw)
            accs = [None if first else mixed[i, js] for i in range(rows)]
            for k in range(rows):
                bk = b2[rr, k, js].astype(F32)
                for i in range(rows):
                    term = af[k * rows + i : k * rows + i + 1, :] * bk
                    accs[i] = term if accs[i] is None else accs[i] + term
            for i in range(rows):
                mixed[i, js] = accs[i]

    incoming(r, True)
    for dz in range(1, nz):
        zz = lax.rem(z + nz - dz, nz)
        rr = zz * 2 + y
        send(b2.at[rr], b2.at[rr], s_b2.at[dz], r_b2.at[rr], rn, c).wait_recv()
        cp = send(b2.at[rr], b2.at[rr], s_f2.at[dz], r_b2.at[rr], rn, c)
        cp.start()
        b2_sends.append(cp)
        incoming(rr, False)
    for dz in range(nz):
        zz = lax.rem(z + nz - dz, nz)
        rr = zz * 2 + (1 - y)
        send(b2.at[rr], b2.at[rr], s_f2.at[dz], r_b2.at[rr], rn, c).wait_recv()
        incoming(rr, False)
    out_ref[...] = finish(1).reshape(rows, cols, width)

    for cp in b_sends + f_sends + b2_sends:
        cp.wait_send()
    a_send.wait_send()

    @pl.when(d != c)
    def _():
        sib_b.wait_send()

    for cp, local in a_sends:
        @pl.when(jnp.logical_not(local))
        def _():
            cp.wait_send()


def shards(nrow, pair, token_mask, chain_ids, chain_bias, in_gain, proj_weight, out_gain, out_weight):
    rows, cols, width = pair.shape
    hidden = out_weight.shape[1]
    half = nrow // 2
    nz = nrow // 2
    vm = pl.BlockSpec(memory_space=pltpu.VMEM)
    sm = pl.BlockSpec(memory_space=pltpu.SMEM)
    dma = pltpu.SemaphoreType.DMA
    block = (rows, cols, hidden)
    return pl.pallas_call(
        functools.partial(kernel, nrow),
        out_shape=jax.ShapeDtypeStruct(pair.shape, BF16),
        in_specs=[vm, sm, sm, vm, vm, vm, vm, vm],
        out_specs=vm,
        scratch_shapes=[
            pltpu.VMEM(pair.shape, F32),
            pltpu.VMEM((rows, cols, width), F32),
            pltpu.VMEM((rows * cols, width), F32),
            pltpu.VMEM(block, F32),
            pltpu.VMEM(block, BF16),
            pltpu.VMEM(block, BF16),
            pltpu.VMEM((2,) + block, BF16),
            pltpu.VMEM((rows, 2 * cols, hidden), F32),
            pltpu.VMEM((half, 2) + block, BF16),
            pltpu.VMEM((cols * rows * 8, hidden), F32),
            pltpu.VMEM((half, rows * rows, hidden), BF16),
            pltpu.VMEM((nrow, rows * rows, hidden), BF16),
            pltpu.VMEM((nrow,) + block, BF16),
            dma((nz,)), dma((nz // 2, 2)), dma((half, 2)), dma, dma,
            dma((half,)), dma((nz,)), dma((nrow,)),
            dma((nz,)), dma((nz,)), dma((nrow,)),
        ],
        compiler_params=pltpu.CompilerParams(
            collective_id=0, has_side_effects=True, vmem_limit_bytes=56 * 2**20
        ),
    )(pair, token_mask, chain_ids, chain_bias.reshape(1, width), in_gain, proj_weight, out_gain, out_weight)


def solution(mesh):
    in_specs = (P(("grp", "row"), "col", None), P("grp"), P("grp"), P(), P(), P(), P(), P())
    out_specs = P(("grp", "row"), "col", None)
    return jax.shard_map(
        functools.partial(shards, mesh.shape["row"]),
        mesh=mesh, in_specs=in_specs, out_specs=out_specs, check_vma=False,
    )
```

time: 143 us -> 36.7 us (0.26)
  blocking collectives: 96 us -> 0 us
  Pallas kernels: 0 us -> 35.1 us
  between operations: 13.6 us -> 0.01 us
  local copies, waits for them, and re-layouts: 10.6 us -> 1.47 us
  other arithmetic: 8.32 us -> 0 us
  waiting for transfers between devices: 8.15 us -> 0 us
  matrix products: 6.33 us -> 0 us
    all_gather x3 -> x0, blocking collectives: 96 us -> none  [the longest x1 33 us: shards(): lax.all_gather(b_out, 'row', axis=0, tiled=True)]
    pallas_call x0 -> x1, Pallas kernels: none -> 35.1 us  [shards(): pl.pallas_call(functools.partial(kernel, nrow), out_shape=jax.ShapeDtypeS...]
    reduce_scatter x1 -> x0, waiting for transfers between devices: 8.09 us -> none  [shards(): lax.psum_scatter(partial_sums, 'col', scatter_dimension=1, tiled=True)]
    dot_general x6 -> x0, matrix products: 6.33 us -> none  [the longest x2 1.97 us: finish(): jnp.dot(mnorm.reshape(-1, hidden), weight_out, preferred_element_type=jnp...]
    all_gather x2 -> x0, local copies, waits for them, and re-layouts: 5.94 us -> none  [the longest x1 2.97 us: shards(): lax.all_gather(b_out, 'row', axis=0, tiled=True)]
    reduce_sum x6 -> x0, other arithmetic: 4.48 us -> none  [the longest x4 2.46 us: layer_norm(): variance = jnp.mean(centred * centred, axis=-1, keepdims=True)]
    convert_element_type x7 -> x0, other arithmetic: 2.99 us -> none  [the longest x2 1.25 us: finish(): mnorm = layer_norm(mixed, gain_out).astype(jnp.bfloat16)]
    mul x2 -> x0, local copies, waits for them, and re-layouts: 1.52 us -> none  [layer_norm(): return centred * lax.rsqrt(variance + 1e-05) * gain]
  transfers between devices with their start and end apart: 2 -> 0, of which waited for: 1 -> 0; matrix products, arithmetic and copies ran while one was open for 3% -> 0% of each run, Pallas kernels for 0% -> 0%
where the time goes in v1:
time: 36.7 us; the launch traced here: 36.5 us
  Pallas kernels  35.1 us (96%)
  local copies, waits for them, and re-layouts  1.47 us (4%)
    pallas_call x1, Pallas kernels, shards(): pl.pallas_call(functools.partial(kernel, nrow), out_shape=jax.ShapeDtypeS...  35.1 us
    unnamed x1, local copies, waits for them, and re-layouts  1.47 us

profile of v1, /device:TPU:0, one launch (start us, length us, event | category | flops | bytes accessed | tf_op | source)
XLA Modules:
  0.0 36.5 jit_solution(1543671517460116761)
XLA Ops:
  0.0 35.1 %shard_map.82 = bf16[8,32,128]{2,1,0:T(8,128)(2,1)} custom-call(bf16[8,32,128]{2,1,0:T(8,128)(2,1)} %pair_ref.1, s32[64]{0:T(128)} %mask_ref.1, s32[64]{0:T(128)} %chain_ref.1, f32[1,128]{1,0:T(1,128)} %bitcast.1, f32[2,128]{1,0:T(2,128)} %gin_ref.1, bf16[2,128,640]{2,1,0:T(8,128)(2,1)} %wp_ref.1, f32[2,128]{1,0:T(2,128)} %gout_ref.1, ...), custom_call_target="tpu_custom_call" | custom-call | tf_op jit(solution)/shard_map/pallas_call | solution.py:260
  35.1 1.5 %copy.10 = bf16[8,32,128]{2,1,0:T(8,128)(2,1)} copy(bf16[8,32,128]{2,1,0:T(8,128)(2,1)} %shard_map.82) | data formatting | bytes 131072

commit v2 on v1

v2 whole, which is shorter than its diff:
```python
import functools
import jax
import jax.numpy as jnp
from jax import lax
from jax.experimental import pallas as pl
from jax.experimental.pallas import tpu as pltpu
from jax.sharding import PartitionSpec as P

F32 = jnp.float32
BF16 = jnp.bfloat16
MESH = pl.DeviceIdType.MESH


def sigmoid(x):
    return 0.5 * jnp.tanh(0.5 * x) + 0.5


def layer_norm(values, gain):
    mean = jnp.mean(values, axis=-1, keepdims=True)
    centred = values - mean
    variance = jnp.mean(centred * centred, axis=-1, keepdims=True)
    return centred * lax.rsqrt(variance + 1e-05) * gain


def kernel(
    nrow,
    pair_ref, mask_ref, chain_ref, bias_ref, gin_ref, wp_ref, gout_ref, wo_ref,
    out_ref,
    state, pm, gate, mixed, own_b, a1, a1f, b1, part, ret, a2s, a2, b2, near, ret2,
    s_b1, r_b1, s_a1, r_a1, s_ret, r_ret, s_a2, s_fa2, r_a2, s_b2, r_b2,
):
    rows, cols, width = pair_ref.shape
    hidden = wo_ref.shape[1]
    nz = nrow // 2
    half = nrow // 2
    grp = lax.axis_index("grp")
    r = lax.axis_index("row")
    c = lax.axis_index("col")
    z, y = r // 2, r % 2
    rn = z * 2 + (1 - y)
    tokens = rows * cols
    d = r // half
    nt = nz // 2
    t_me = z % nt

    def send(src, dst, ss, rs, row, col):
        return pltpu.make_async_remote_copy(
            src_ref=src, dst_ref=dst, send_sem=ss, recv_sem=rs,
            device_id=(grp, row, col), device_id_type=MESH,
        )

    barrier = pltpu.get_barrier_semaphore()

    def greet(row, col):
        pl.semaphore_signal(barrier, inc=1, device_id=(grp, row, col), device_id_type=MESH)

    greet(r, 1 - c)
    greet(rn, c)
    for dz in range(1, nz):
        tz = lax.rem(z + dz, nz)
        greet(tz * 2 + y, c)

        @pl.when((tz * 2 + y) // half == c)
        def _():
            greet(tz * 2 + y, 1 - c)

    peers = 2 + (nz - 1) * jnp.where(d == c, 1, 2)

    lane_rows = lax.broadcasted_iota(jnp.int32, (8, width), 0)
    for jb in range(cols // 8):
        mcol = jnp.zeros((8, width), jnp.int32)
        ccol = jnp.zeros((8, width), jnp.int32)
        for s in range(8):
            at = c * cols + jb * 8 + s
            mcol = jnp.where(lane_rows == s, mask_ref[at], mcol)
            ccol = jnp.where(lane_rows == s, chain_ref[at], ccol)
        mcol = mcol.astype(F32)
        js = slice(jb * 8, jb * 8 + 8)
        for i in range(rows):
            mi = mask_ref[r * rows + i].astype(F32)
            pm[i, js] = mcol * mi
            same = (ccol == chain_ref[r * rows + i]).astype(F32)
            state[i, js] = pair_ref[i, js].astype(F32) + same * bias_ref[...]

    def normed_of(l):
        zs = state[...].reshape(tokens, width)
        return layer_norm(zs, gin_ref[l : l + 1, :]).astype(BF16)

    def side(normed, l, at):
        pr = jnp.dot(normed, wp_ref[l, :, at : at + 2 * hidden], preferred_element_type=F32)
        return pm[...].reshape(tokens, width) * sigmoid(pr[:, hidden:]) * pr[:, :hidden]

    def gate_of(normed, l):
        pr = jnp.dot(normed, wp_ref[l, :, 4 * hidden :], preferred_element_type=F32)
        gate[...] = sigmoid(pr)

    def finish(l):
        mn = layer_norm(mixed[...].reshape(tokens, hidden), gout_ref[l : l + 1, :]).astype(BF16)
        change = jnp.dot(mn, wo_ref[l], preferred_element_type=F32)
        res = state[...].reshape(tokens, width) + gate[...] * change
        return res.astype(BF16)

    normed = normed_of(0)
    own_b[...] = side(normed, 0, 2 * hidden).astype(BF16).reshape(rows, cols, hidden)
    pl.semaphore_wait(barrier, peers)

    sends = []
    for dz in range(1, nz):
        tz = lax.rem(z + dz, nz)
        cp = send(own_b, b1.at[t_me, c], s_b1.at[dz], r_b1.at[t_me, c], tz * 2 + y, d)
        cp.start()
        sends.append(cp)
    sib_b = send(own_b, b1.at[t_me, c], s_b1.at[0], r_b1.at[t_me, c], r, 1 - c)

    @pl.when(d != c)
    def _():
        sib_b.start()

    @pl.when(d == c)
    def _():
        b1[t_me, c] = own_b[...]

    a1[0, c] = side(normed, 0, 0).astype(BF16).reshape(rows, cols, hidden)
    near_a = send(a1.at[0, c], a1.at[1, c], s_a1.at[0], r_a1.at[0], rn, c)
    near_a.start()
    own_a = send(a1.at[0, c], a1.at[0, c], s_a1.at[1], r_a1.at[1], r, 1 - c)
    own_a.start()
    gate_of(normed, 0)
    near_a.wait_recv()
    far_a = send(a1.at[1, c], a1.at[1, c], s_a1.at[2], r_a1.at[2], r, 1 - c)
    far_a.start()
    sends += [near_a, own_a, far_a]
    own_a.wait_recv()
    far_a.wait_recv()
    for p in range(2):
        for cc in range(2):
            a1f[p, :, cc * cols : (cc + 1) * cols, :] = a1[p, cc].astype(F32)

    kb_n = 2 * cols // 8
    nj = nt * rows

    def outgoing(p, t):
        def body(j, carry):
            b0 = b1[t, 0, j].astype(F32)
            bb1 = b1[t, 1, j].astype(F32)
            bs = [b0[kb * 8 : kb * 8 + 8] for kb in range(kb_n // 2)]
            bs += [bb1[kb * 8 : kb * 8 + 8] for kb in range(kb_n // 2)]
            base = pl.multiple_of((t * rows + j) * (rows * 8), rows * 8)
            for i in range(rows):
                acc = a1f[p, i, 0:8] * bs[0]
                for kb in range(1, kb_n):
                    acc = acc + a1f[p, i, kb * 8 : kb * 8 + 8] * bs[kb]
                part[p, pl.ds(base + i * 8, 8), :] = acc
            return carry
        lax.fori_loop(0, rows, body, 0)

    def total(p, i):
        tot = part[p, pl.ds(i * 8, nj, stride=rows * 8), :]
        for k in range(1, 8):
            tot = tot + part[p, pl.ds(i * 8 + k, nj, stride=rows * 8), :]
        return tot

    for k in range(nt):
        t = lax.rem(t_me + k, nt)
        mine = (c * nt + t) == z
        for cc in range(2):
            @pl.when(jnp.logical_not(jnp.logical_and(mine, c == cc)))
            def _():
                send(b1.at[t, cc], b1.at[t, cc], s_b1.at[0], r_b1.at[t, cc], rn, c).wait_recv()
        outgoing(1, t)
    for i in range(rows):
        ret[0, i] = total(1, i).astype(BF16)
    back = send(ret.at[0], ret.at[1], s_ret.at[0], r_ret.at[0], rn, c)
    back.start()
    sends.append(back)
    for t in range(nt):
        outgoing(0, t)
    for i in range(rows):
        tot = total(0, i)
        for t in range(nt):
            at = pl.multiple_of((t * 2 + y) * rows, rows)
            mixed[i, pl.ds(at, rows)] = tot[t * rows : (t + 1) * rows]
    back.wait_recv()
    for i in range(rows):
        tot = ret[1, i].astype(F32)
        for t in range(nt):
            at = pl.multiple_of((t * 2 + 1 - y) * rows, rows)
            mixed[i, pl.ds(at, rows)] = tot[t * rows : (t + 1) * rows]
    state[...] = finish(0).astype(F32).reshape(rows, cols, width)

    normed = normed_of(1)
    a_side = side(normed, 1, 0).reshape(rows, cols, hidden)
    sq = rows * rows
    for t in range(nt):
        for p in range(2):
            q = t * 2 + p
            a2s[t, p * sq : (p + 1) * sq] = (
                a_side[:, q * rows : (q + 1) * rows, :].reshape(sq, hidden).astype(BF16)
            )
    a_sends = []
    for k in range(nt):
        t = lax.rem(t_me + k, nt)
        tz = c * nt + t
        cp = send(a2s.at[t], a2.at[z], s_a2.at[k], r_a2.at[z], tz * 2 + y, c)

        @pl.when(tz != z)
        def _():
            cp.start()

        @pl.when(tz == z)
        def _():
            a2[z] = a2s[t]
        a_sends.append((cp, tz != z))
    b2[z] = side(normed, 1, 2 * hidden).astype(BF16).reshape(rows, cols, hidden)
    for dz in range(1, nz):
        tz = lax.rem(z + dz, nz)
        cp = send(b2.at[z], b2.at[z], s_b2.at[dz], r_b2.at[z], tz * 2 + y, c)
        cp.start()
        sends.append(cp)
    gate_of(normed, 1)

    def hop(t):
        zz = lax.rem(z + t, nz)
        return send(a2.at[zz], a2.at[zz], s_fa2.at[t], r_a2.at[zz], r, 1 - c)

    @pl.when(d == c)
    def _():
        for t in range(nz):
            if t:
                hop(t).wait_recv()
            hop(t).start()

    @pl.when(d != c)
    def _():
        for t in range(nz):
            hop(t).wait_recv()

    jw = min(cols, 32)

    def incoming(dst, p, zz, first):
        af = a2[zz, pl.ds(pl.multiple_of(p * sq, sq), sq)].astype(F32)
        for jb in range(cols // jw):
            js = slice(jb * jw, (jb + 1) * jw)
            accs = [None if first else dst[i, js] for i in range(rows)]
            for k in range(rows):
                bk = b2[zz, k, js].astype(F32)
                for i in range(rows):
                    term = af[k * rows + i : k * rows + i + 1, :] * bk
                    accs[i] = term if accs[i] is None else accs[i] + term
            for i in range(rows):
                dst[i, js] = accs[i]

    for dz in range(nz):
        zz = lax.rem(z + nz - dz, nz)
        if dz:
            send(b2.at[zz], b2.at[zz], s_b2.at[dz], r_b2.at[zz], rn, c).wait_recv()
        incoming(near, 1 - y, zz, dz == 0)
        if dz < nz - 1:
            incoming(mixed, y, zz, dz == 0)
    ret2[0] = near[...].astype(BF16)
    back2 = send(ret2.at[0], ret2.at[1], s_ret.at[1], r_ret.at[1], rn, c)
    back2.start()
    sends.append(back2)
    incoming(mixed, y, lax.rem(z + 1, nz), False)
    back2.wait_recv()
    mixed[...] = mixed[...] + ret2[1].astype(F32)
    out_ref[...] = finish(1).reshape(rows, cols, width)

    for cp in sends:
        cp.wait_send()

    @pl.when(d != c)
    def _():
        sib_b.wait_send()

    @pl.when(d == c)
    def _():
        for t in range(nz):
            hop(t).wait_send()

    for cp, remote in a_sends:
        @pl.when(remote)
        def _():
            cp.wait_send()


def shards(nrow, pair, token_mask, chain_ids, chain_bias, in_gain, proj_weight, out_gain, out_weight):
    rows, cols, width = pair.shape
    hidden = out_weight.shape[1]
    nz = nrow // 2
    nt = nz // 2
    vm = pl.BlockSpec(memory_space=pltpu.VMEM)
    sm = pl.BlockSpec(memory_space=pltpu.SMEM)
    dma = pltpu.SemaphoreType.DMA
    block = (rows, cols, hidden)
    return pl.pallas_call(
        functools.partial(kernel, nrow),
        out_shape=jax.ShapeDtypeStruct(pair.shape, BF16),
        in_specs=[vm, sm, sm, vm, vm, vm, vm, vm],
        out_specs=vm,
        scratch_shapes=[
            pltpu.VMEM(pair.shape, F32),
            pltpu.VMEM((rows, cols, width), F32),
            pltpu.VMEM((rows * cols, width), F32),
            pltpu.VMEM(block, F32),
            pltpu.VMEM(block, BF16),
            pltpu.VMEM((2, 2) + block, BF16),
            pltpu.VMEM((2, rows, 2 * cols, hidden), F32),
            pltpu.VMEM((nt, 2) + block, BF16),
            pltpu.VMEM((2, nt * rows * rows * 8, hidden), F32),
            pltpu.VMEM((2, rows, nt * rows, hidden), BF16),
            pltpu.VMEM((nt, 2 * rows * rows, hidden), BF16),
            pltpu.VMEM((nz, 2 * rows * rows, hidden), BF16),
            pltpu.VMEM((nz,) + block, BF16),
            pltpu.VMEM(block, F32),
            pltpu.VMEM((2,) + block, BF16),
            dma((nz,)), dma((nt, 2)), dma((3,)), dma((3,)), dma((2,)), dma((2,)),
            dma((nt,)), dma((nz,)), dma((nz,)),
            dma((nz,)), dma((nz,)),
        ],
        compiler_params=pltpu.CompilerParams(
            collective_id=0, has_side_effects=True, vmem_limit_bytes=56 * 2**20
        ),
    )(pair, token_mask, chain_ids, chain_bias.reshape(1, width), in_gain, proj_weight, out_gain, out_weight)


def solution(mesh):
    in_specs = (P(("grp", "row"), "col", None), P("grp"), P("grp"), P(), P(), P(), P(), P())
    out_specs = P(("grp", "row"), "col", None)
    return jax.shard_map(
        functools.partial(shards, mesh.shape["row"]),
        mesh=mesh, in_specs=in_specs, out_specs=out_specs, check_vma=False,
    )
```

time: 36.7 us -> 30.3 us (0.83)
  Pallas kernels: 35.1 us -> 28.7 us
    pallas_call x1, Pallas kernels: 35.1 us -> 28.7 us  [shards(): pl.pallas_call(functools.partial(kernel, nrow), out_shape=jax.ShapeDtypeS...]
where the time goes in v2:
time: 30.3 us; the launch traced here: 30.1 us
  Pallas kernels  28.7 us (95%)
  local copies, waits for them, and re-layouts  1.47 us (5%)
    pallas_call x1, Pallas kernels, shards(): pl.pallas_call(functools.partial(kernel, nrow), out_shape=jax.ShapeDtypeS...  28.7 us
    unnamed x1, local copies, waits for them, and re-layouts  1.47 us

profile of v2, /device:TPU:0, one launch (start us, length us, event | category | flops | bytes accessed | tf_op | source)
XLA Modules:
  0.0 30.1 jit_solution(18133752314715097479)
XLA Ops:
  0.0 28.7 %shard_map.82 = bf16[8,32,128]{2,1,0:T(8,128)(2,1)} custom-call(bf16[8,32,128]{2,1,0:T(8,128)(2,1)} %pair_ref.1, s32[64]{0:T(128)} %mask_ref.1, s32[64]{0:T(128)} %chain_ref.1, f32[1,128]{1,0:T(1,128)} %bitcast.1, f32[2,128]{1,0:T(2,128)} %gin_ref.1, bf16[2,128,640]{2,1,0:T(8,128)(2,1)} %wp_ref.1, f32[2,128]{1,0:T(2,128)} %gout_ref.1, ...), custom_call_target="tpu_custom_call" | custom-call | tf_op jit(solution)/shard_map/pallas_call | solution.py:296
  28.7 1.5 %copy.10 = bf16[8,32,128]{2,1,0:T(8,128)(2,1)} copy(bf16[8,32,128]{2,1,0:T(8,128)(2,1)} %shard_map.82) | data formatting | bytes 131072

commit v3 on v2

--- a/solution.py
+++ b/solution.py
@@ -211,12 +211,16 @@
         def _():
             a2[z] = a2s[t]
         a_sends.append((cp, tz != z))
-    b2[z] = side(normed, 1, 2 * hidden).astype(BF16).reshape(rows, cols, hidden)
-    for dz in range(1, nz):
-        tz = lax.rem(z + dz, nz)
-        cp = send(b2.at[z], b2.at[z], s_b2.at[dz], r_b2.at[z], tz * 2 + y, c)
-        cp.start()
-        sends.append(cp)
+    hc = cols // 2
+    b_side = side(normed, 1, 2 * hidden).reshape(rows, cols, hidden)
+    for h in range(2):
+        b2[z, h] = b_side[:, h * hc : (h + 1) * hc, :].astype(BF16)
+    for h in range(2):
+        for dz in range(1, nz):
+            tz = lax.rem(z + dz, nz)
+            cp = send(b2.at[z, h], b2.at[z, h], s_b2.at[dz, h], r_b2.at[z, h], tz * 2 + y, c)
+            cp.start()
+            sends.append(cp)
     gate_of(normed, 1)
 
     def hop(t):
@@ -235,35 +239,40 @@
         for t in range(nz):
             hop(t).wait_recv()
 
-    jw = min(cols, 32)
-
-    def incoming(dst, p, zz, first):
+    jw = min(hc, 32)
+
+    def incoming(dst, p, zz, h, first):
         af = a2[zz, pl.ds(pl.multiple_of(p * sq, sq), sq)].astype(F32)
-        for jb in range(cols // jw):
+        for jb in range(hc // jw):
             js = slice(jb * jw, (jb + 1) * jw)
-            accs = [None if first else dst[i, js] for i in range(rows)]
+            to = slice(h * hc + jb * jw, h * hc + (jb + 1) * jw)
+            accs = [None if first else dst[i, to] for i in range(rows)]
             for k in range(rows):
-                bk = b2[zz, k, js].astype(F32)
+                bk = b2[zz, h, k, js].astype(F32)
                 for i in range(rows):
                     term = af[k * rows + i : k * rows + i + 1, :] * bk
                     accs[i] = term if accs[i] is None else accs[i] + term
             for i in range(rows):
-                dst[i, js] = accs[i]
-
-    for dz in range(nz):
-        zz = lax.rem(z + nz - dz, nz)
-        if dz:
-            send(b2.at[zz], b2.at[zz], s_b2.at[dz], r_b2.at[zz], rn, c).wait_recv()
-        incoming(near, 1 - y, zz, dz == 0)
-        if dz < nz - 1:
-            incoming(mixed, y, zz, dz == 0)
-    ret2[0] = near[...].astype(BF16)
-    back2 = send(ret2.at[0], ret2.at[1], s_ret.at[1], r_ret.at[1], rn, c)
-    back2.start()
-    sends.append(back2)
-    incoming(mixed, y, lax.rem(z + 1, nz), False)
-    back2.wait_recv()
-    mixed[...] = mixed[...] + ret2[1].astype(F32)
+                dst[i, to] = accs[i]
+
+    backs = []
+    for h in range(2):
+        for dz in range(nz):
+            zz = lax.rem(z + nz - dz, nz)
+            if dz:
+                send(b2.at[zz, h], b2.at[zz, h], s_b2.at[dz, h], r_b2.at[zz, h], rn, c).wait_recv()
+            incoming(near, 1 - y, zz, h, dz == 0)
+        ret2[0, h] = near[:, h * hc : (h + 1) * hc, :].astype(BF16)
+        back2 = send(ret2.at[0, h], ret2.at[1, h], s_ret.at[1 + h], r_ret.at[1 + h], rn, c)
+        back2.start()
+        sends.append(back2)
+        backs.append(back2)
+        for dz in range(nz):
+            incoming(mixed, y, lax.rem(z + nz - dz, nz), h, dz == 0)
+    for h in range(2):
+        to = slice(h * hc, (h + 1) * hc)
+        backs[h].wait_recv()
+        mixed[:, to, :] = mixed[:, to, :] + ret2[1, h].astype(F32)
     out_ref[...] = finish(1).reshape(rows, cols, width)
 
     for cp in sends:
@@ -311,12 +320,12 @@
             pltpu.VMEM((2, rows, nt * rows, hidden), BF16),
             pltpu.VMEM((nt, 2 * rows * rows, hidden), BF16),
             pltpu.VMEM((nz, 2 * rows * rows, hidden), BF16),
-            pltpu.VMEM((nz,) + block, BF16),
+            pltpu.VMEM((nz, 2, rows, cols // 2, hidden), BF16),
             pltpu.VMEM(block, F32),
-            pltpu.VMEM((2,) + block, BF16),
-            dma((nz,)), dma((nt, 2)), dma((3,)), dma((3,)), dma((2,)), dma((2,)),
+            pltpu.VMEM((2, 2, rows, cols // 2, hidden), BF16),
+            dma((nz,)), dma((nt, 2)), dma((3,)), dma((3,)), dma((3,)), dma((3,)),
             dma((nt,)), dma((nz,)), dma((nz,)),
-            dma((nz,)), dma((nz,)),
+            dma((nz, 2)), dma((nz, 2)),
         ],
         compiler_params=pltpu.CompilerParams(
             collective_id=0, has_side_effects=True, vmem_limit_bytes=56 * 2**20

time: 30.3 us -> 29.8 us (0.983)
  Pallas kernels: 28.7 us -> 28.1 us
    pallas_call x1, Pallas kernels: 28.7 us -> 28.1 us  [shards(): pl.pallas_call(functools.partial(kernel, nrow), out_shape=jax.ShapeDtypeS...]
where the time goes in v3:
time: 29.8 us; the launch traced here: 29.6 us
  Pallas kernels  28.1 us (94%)
  local copies, waits for them, and re-layouts  1.47 us (5%)
    pallas_call x1, Pallas kernels, shards(): pl.pallas_call(functools.partial(kernel, nrow), out_shape=jax.ShapeDtypeS...  28.1 us
    unnamed x1, local copies, waits for them, and re-layouts  1.47 us

profile of v3, /device:TPU:0, one launch (start us, length us, event | category | flops | bytes accessed | tf_op | source)
XLA Modules:
  0.0 29.6 jit_solution(14575944769890931736)
XLA Ops:
  0.0 28.1 %shard_map.82 = bf16[8,32,128]{2,1,0:T(8,128)(2,1)} custom-call(bf16[8,32,128]{2,1,0:T(8,128)(2,1)} %pair_ref.1, s32[64]{0:T(128)} %mask_ref.1, s32[64]{0:T(128)} %chain_ref.1, f32[1,128]{1,0:T(1,128)} %bitcast.1, f32[2,128]{1,0:T(2,128)} %gin_ref.1, bf16[2,128,640]{2,1,0:T(8,128)(2,1)} %wp_ref.1, f32[2,128]{1,0:T(2,128)} %gout_ref.1, ...), custom_call_target="tpu_custom_call" | custom-call | tf_op jit(solution)/shard_map/pallas_call | solution.py:305
  28.2 1.5 %copy.10 = bf16[8,32,128]{2,1,0:T(8,128)(2,1)} copy(bf16[8,32,128]{2,1,0:T(8,128)(2,1)} %shard_map.82) | data formatting | bytes 131072

commit v4 on v3

--- a/solution.py
+++ b/solution.py
@@ -102,6 +102,8 @@
 
     normed = normed_of(0)
     own_b[...] = side(normed, 0, 2 * hidden).astype(BF16).reshape(rows, cols, hidden)
+    a1[0, c] = side(normed, 0, 0).astype(BF16).reshape(rows, cols, hidden)
+    gate_of(normed, 0)
     pl.semaphore_wait(barrier, peers)
 
     sends = []
@@ -120,12 +122,10 @@
     def _():
         b1[t_me, c] = own_b[...]
 
-    a1[0, c] = side(normed, 0, 0).astype(BF16).reshape(rows, cols, hidden)
     near_a = send(a1.at[0, c], a1.at[1, c], s_a1.at[0], r_a1.at[0], rn, c)
     near_a.start()
     own_a = send(a1.at[0, c], a1.at[0, c], s_a1.at[1], r_a1.at[1], r, 1 - c)
     own_a.start()
-    gate_of(normed, 0)
     near_a.wait_recv()
     far_a = send(a1.at[1, c], a1.at[1, c], s_a1.at[2], r_a1.at[2], r, 1 - c)
     far_a.start()

time: 29.8 us -> 29.8 us (level)
  no operation moved by 1% of the time
where the time goes in v4:
time: 29.8 us; the launch traced here: 29.6 us
  Pallas kernels  28.1 us (94%)
  local copies, waits for them, and re-layouts  1.47 us (5%)
    pallas_call x1, Pallas kernels, shards(): pl.pallas_call(functools.partial(kernel, nrow), out_shape=jax.ShapeDtypeS...  28.1 us
    unnamed x1, local copies, waits for them, and re-layouts  1.47 us

profile of v4, /device:TPU:0, one launch (start us, length us, event | category | flops | bytes accessed | tf_op | source)
XLA Modules:
  0.0 29.6 jit_solution(15044002054449510269)
XLA Ops:
  0.0 28.1 %shard_map.82 = bf16[8,32,128]{2,1,0:T(8,128)(2,1)} custom-call(bf16[8,32,128]{2,1,0:T(8,128)(2,1)} %pair_ref.1, s32[64]{0:T(128)} %mask_ref.1, s32[64]{0:T(128)} %chain_ref.1, f32[1,128]{1,0:T(1,128)} %bitcast.1, f32[2,128]{1,0:T(2,128)} %gin_ref.1, bf16[2,128,640]{2,1,0:T(8,128)(2,1)} %wp_ref.1, f32[2,128]{1,0:T(2,128)} %gout_ref.1, ...), custom_call_target="tpu_custom_call" | custom-call | tf_op jit(solution)/shard_map/pallas_call | solution.py:305
  28.1 1.5 %copy.10 = bf16[8,32,128]{2,1,0:T(8,128)(2,1)} copy(bf16[8,32,128]{2,1,0:T(8,128)(2,1)} %shard_map.82) | data formatting | bytes 131072
